TPU v7x, 32 devices: a whole 2x2x4 slice. The times are simulated.
32 devices in a mesh: seq: 8 (over y, x, core), chan: 4 (over z).
Axes of the slice: x: 2, y: 2, z: 4, core: 2. Of those that a mesh axis runs over, the one named last changes fastest.
Arguments:
- streams: bfloat16 [5, 2048, 8192], P(None, 'seq', 'chan'), may hold values from -6 to 6
- short_filter: bfloat16 [7, 8192], P(None, 'chan'), may hold values from -2 to 2
- long_filter: bfloat16 [128, 8192], P(None, 'chan'), may hold values from -0.5 to 0.5
- edit_table: bfloat16 [16, 8, 8192], P('seq', None, 'chan'), may hold values from -0.25 to 0.25
- edit_bias: float32 [16, 4], replicated, may hold values from -8 to 8
- seq_tiles: int32 [4], replicated, may hold values from 1 to 8, 16 in all
- seq_tenant: int32 [4], replicated, may hold values from 0 to 15
Outputs:
- edited: bfloat16 [2048, 8192], P('seq', 'chan')
Inputs may be any that keep to these rules, and one draw needn't show every extreme that they name: `seq_tiles`: each sequence fills whole tiles; the sequences fill all 16 tiles in order and the longest has 8.
All inputs are finite; a program needn't handle non-finite values.
Results may differ from a plain program's by a relative error of at most 0.013.
Values may be sent and summed in bfloat16 or wider, within the bound.
A program may use at most 64 MiB of HBM per device.

v0:
```python
import jax
import jax.numpy as jnp
from jax import lax
from jax.sharding import PartitionSpec as P

TILE_ROWS = 128
SEQS = 4


def from_behind(block, axis, distance):
    devices = range(lax.axis_size(axis))
    route = [(i - distance, i) for i in devices if i - distance in devices]
    return lax.ppermute(block, axis, route)


def depth_conv(window, taps_filter):
    width = window.shape[-1]
    kernel = taps_filter[::-1][:, None, :]
    return lax.conv_general_dilated(
        window,
        kernel,
        (1,),
        "VALID",
        dimension_numbers=("NWC", "WIO", "NWC"),
        feature_group_count=width,
        preferred_element_type=jnp.float32,
    )


def tiled_conv(field, border, starts, taps_filter):
    rows_here, width = field.shape
    reach = taps_filter.shape[0]
    tile_count = rows_here // TILE_ROWS
    tiles = field.reshape(tile_count, TILE_ROWS, width)
    trailing = tiles[:, TILE_ROWS - (reach - 1) :, :]
    earlier = jnp.concatenate([border[None], trailing[:-1]], axis=0)
    earlier = jnp.where(starts[:, None, None], jnp.zeros_like(earlier), earlier)
    window = jnp.concatenate([earlier, tiles], axis=1)
    return depth_conv(window, taps_filter).reshape(rows_here, width)


def on_device(streams, short_filter, long_filter, edit_table, edit_bias, seq_tiles, seq_tenant):
    rows_here = streams.shape[1]
    width = streams.shape[2]
    short_reach = short_filter.shape[0]
    long_reach = long_filter.shape[0]
    tile_count = rows_here // TILE_ROWS
    seq_ends = jnp.cumsum(seq_tiles)
    first_tile = lax.axis_index("seq") * tile_count
    tile_ids = first_tile + jnp.arange(tile_count, dtype=jnp.int32)
    seq_of = jnp.sum((seq_ends[None, :] <= tile_ids[:, None]).astype(jnp.int32), axis=1)
    starts = (tile_ids == 0) | jnp.any(seq_ends[None, :] == tile_ids[:, None], axis=1)
    first_gate = streams[0]
    first_key = streams[1]
    second_gate = streams[3]
    second_key = streams[4]
    gated = (first_key.astype(jnp.float32) * streams[2].astype(jnp.float32)).astype(jnp.bfloat16)
    short_border = from_behind(gated[rows_here - (short_reach - 1) :], "seq", 1)
    short_out = tiled_conv(gated, short_border, starts, short_filter)
    mixed = (first_gate.astype(jnp.float32) * short_out).astype(jnp.bfloat16)
    carried = (second_key.astype(jnp.float32) * mixed.astype(jnp.float32)).astype(jnp.bfloat16)
    long_border = from_behind(carried[rows_here - (long_reach - 1) :], "seq", 1)
    long_out = tiled_conv(carried, long_border, starts, long_filter)
    hidden = (second_gate.astype(jnp.float32) * long_out).astype(jnp.bfloat16)
    rows_per = edit_table.shape[1]
    rank = rows_per // 2
    all_rows = lax.all_gather(edit_table, "seq", axis=0, tiled=True)
    tenant_count = all_rows.shape[0]
    picker = (seq_tenant[:, None] == jnp.arange(tenant_count, dtype=jnp.int32)[None, :]).astype(
        jnp.bfloat16
    )
    chosen = jnp.dot(
        picker, all_rows.reshape(tenant_count, rows_per * width), preferred_element_type=jnp.float32
    )
    chosen = chosen.astype(jnp.bfloat16).reshape(SEQS, rows_per, width)
    tok_seq = jnp.repeat(seq_of, TILE_ROWS)
    seq_onehot = (tok_seq[:, None] == jnp.arange(SEQS, dtype=jnp.int32)[None, :]).astype(
        jnp.float32
    )
    projected = jnp.dot(
        hidden, chosen.reshape(SEQS * rows_per, width).T, preferred_element_type=jnp.float32
    )
    projected = projected.reshape(rows_here, SEQS, rows_per)
    selected = jnp.sum(projected * seq_onehot[:, :, None], axis=1)
    summed = lax.psum(selected, "chan")
    tenant_total = edit_bias.shape[0]
    bias_pick = (seq_tenant[:, None] == jnp.arange(tenant_total, dtype=jnp.int32)[None, :]).astype(
        jnp.float32
    )
    bias_seq = jnp.dot(bias_pick, edit_bias, precision=lax.Precision.HIGHEST)
    bias_tok = jnp.dot(seq_onehot, bias_seq, precision=lax.Precision.HIGHEST)
    coefficient = summed[:, rank:] - summed[:, :rank] + bias_tok
    spread = (seq_onehot[:, :, None] * coefficient[:, None, :]).reshape(rows_here, SEQS * rank)
    rows_r = chosen[:, :rank, :].reshape(SEQS * rank, width).astype(jnp.float32)
    change = jnp.dot(spread, rows_r, precision=lax.Precision.HIGHEST)
    return (hidden.astype(jnp.float32) + change).astype(jnp.bfloat16)


def solution(mesh):
    in_specs = (
        P(None, "seq", "chan"),
        P(None, "chan"),
        P(None, "chan"),
        P("seq", None, "chan"),
        P(),
        P(),
        P(),
    )
    out_specs = P("seq", "chan")
    return jax.shard_map(
        on_device, mesh=mesh, in_specs=in_specs, out_specs=out_specs, check_vma=False
    )
```

profile of v0, /device:TPU:4, one launch (start us, length us, event | category | flops | bytes accessed | tf_op | source)
XLA Modules:
  0.0 94.1 jit_solution(3191929265231927188)
XLA Ops:
  0.0 0.0 copy-start
  0.0 1.9 %multiply_convert_fusion.3 = bf16[1,256,2048]{2,1,0:T(8,128)(2,1)S(1)} fusion(bf16[5,256,2048]{2,1,0:T(8,128)(2,1)} %param.7), kind=kLoop, calls=%fused_computation.12 | loop fusion | flops 2097152 | bytes 3145728 | tf_op jit(solution)/shard_map/convert_element_type | solution.py:57
  2.0 1.9 %collective-permute-start = (bf16[6,2048]{1,0:T(8,128)(2,1)S(1)}, bf16[6,2048]{1,0:T(8,128)(2,1)S(1)}, u32[]{:S(2)}, u32[]{:S(2)}) collective-permute-start(bf16[6,2048]{1,0:T(8,128)(2,1)S(1)} %slice_bitcast_fusion), channel_id=1, source_target_pairs={{0,4},{4,8},{8,12},{12,16},{16,20},{20,24},{24,28},{1,5},{5,9},{9,... | collective-permute-start | bytes 73736 | tf_op jit(solution)/shard_map/ppermute | solution.py:13
  3.9 0.0 copy-start.8
  3.9 0.0 copy-start.5
  3.9 0.0 copy-start.7
  3.9 6.3 %slice_convert_fusion.2 = (f32[1,256,2048]{2,1,0:T(8,128)}, f32[256,2048]{1,0:T(8,128)}, f32[256,2048]{1,0:T(8,128)}, f32[1,256,2048]{2,1,0:T(8,128)}, f32[1,256,2048]{2,1,0:T(8,128)}) fusion(bf16[5,256,2048]{2,1,0:T(8,128)(2,1)} %param.7), kind=kLoop, calls=%fused_computation.30 | loop fusion | flops 1572864 | bytes 13631488 | tf_op jit(solution)/shard_map/convert_element_type | solution.py:64
  10.3 0.0 copy-done.8
  10.3 0.2 reduce-window.8
  10.5 0.2 compare_reduce_fusion
  10.7 0.0 copy-done.5
  10.7 9.9 %all_gather.3 = bf16[16,8,2048]{2,1,0:T(8,128)(2,1)S(1)} all-gather(bf16[2,8,2048]{2,1,0:T(8,128)(2,1)S(1)} %copy-done.5), channel_id=1, replica_groups=mesh['seq'=8,'chan'=4] {'seq'}, dimensions={0}, use_global_device_ids=true | all-gather | bytes 589824 | tf_op jit(solution)/shard_map/all_gather | solution.py:67
  20.6 0.3 copy.73
  20.9 0.3 convolution_convert_fusion
  21.2 0.2 fusion.22
  21.4 0.4 rev.6
  21.9 0.0 collective-permute-done
  21.9 0.1 maximum_select_fusion.1
  21.9 0.3 pad_maximum_fusion.1
  22.3 1.1 %copy.72 = bf16[2,134,2048]{2,0,1:T(2,128)(2,1)S(1)} copy(bf16[2,134,2048]{2,1,0:T(8,128)(2,1)S(1)} %pad_maximum_fusion.1) | data formatting | bytes 2195456
  23.4 0.9 pad.clone
  24.3 0.0 copy-start.9
  24.3 0.3 slice.60
  24.6 3.9 %fusion.5 = bf16[2,8,23,2048]{3,0,2,1:T(2,128)(2,1)S(1)} fusion(bf16[2,7,6,2048]{3,0,2,1:T(2,128)(2,1)S(1)} %slice.60, bf16[2,8,17,2048]{3,0,2,1:T(2,128)(2,1)S(1)} %bitcast.53), kind=kLoop, calls=%fused_computation.15 | loop fusion | flops 4521984 | bytes 2965504 | tf_op jit(solution)/shard_map/conv_general_dilated | solution.py:19
  28.4 1.4 %convolution_select_fusion = f32[16,17,2048]{2,0,1:T(8,128)S(1)} fusion(bf16[2,8,23,2048]{3,0,2,1:T(2,128)(2,1)S(1)} %fusion.5, pred[16,17]{0,1:T(8,128)(4,1)S(1)} %copy-done.9, bf16[7,1,2048]{2,0,1:T(8,128)(2,1)S(1)} %bitcast.65), kind=kOutput, calls=%fused_computation.5 | convolution fusion | flops 8355840 | bytes 3764496 | tf_op jit(solution)/shard_map/conv_general_dilated | solution.py:19
  29.8 1.4 %copy.67 = f32[16,17,2048]{2,1,0:T(8,128)S(1)} copy(f32[16,17,2048]{2,0,1:T(8,128)S(1)} %convolution_select_fusion) | data formatting | bytes 4456448 | tf_op jit(solution)/shard_map/conv_general_dilated | solution.py:19
  31.2 1.6 %reshape.118 = f32[2,136,2048]{2,1,0:T(8,128)} reshape(f32[16,17,2048]{2,1,0:T(8,128)S(1)} %copy.67) | data formatting | bytes 4456448 | tf_op jit(solution)/shard_map/conv_general_dilated | solution.py:19
  32.7 3.6 %fusion.25 = (f32[2,128,2048]{2,1,0:T(8,128)S(1)}, bf16[2,128,2048]{2,1,0:T(8,128)(2,1)S(1)}) fusion(f32[2,136,2048]{2,1,0:T(8,128)} %reshape.118, f32[2,128,2048]{2,1,0:T(8,128)} %bitcast.50, f32[2,128,2048]{2,1,0:T(8,128)} %bitcast.51), kind=kLoop, calls=%fused_computation.55 | loop fusion | flops 2621440 | bytes 9437184 | tf_op jit(solution)/shard_map/conv_general_dilated | solution.py:19
  36.4 0.0 copy-start.4
  36.4 0.4 copy-done.3
  36.8 0.3 fusion.9
  37.2 2.4 %collective-permute-start.1 = (bf16[127,2048]{1,0:T(8,128)(2,1)S(1)}, bf16[127,2048]{1,0:T(8,128)(2,1)S(1)}, u32[]{:S(2)}, u32[]{:S(2)}) collective-permute-start(bf16[127,2048]{1,0:T(8,128)(2,1)S(1)} %fusion.9), channel_id=1, source_target_pairs={{0,4},{4,8},{8,12},{12,16},{16,20},{20,24},{24,28},{1,5},{5,9},{9,... | collective-permute-start | bytes 1560584 | tf_op jit(solution)/shard_map/ppermute | solution.py:13
  39.6 0.1 broadcast_bitcast_fusion
  39.7 0.6 rev.7
  40.3 0.1 copy.89
  40.4 0.0 copy-done
  40.4 0.2 fusion.20
  40.6 0.1 slice.65
  40.7 7.8 %collective-permute-done.1 = bf16[127,2048]{1,0:T(8,128)(2,1)S(1)} collective-permute-done((bf16[127,2048]{1,0:T(8,128)(2,1)S(1)}, bf16[127,2048]{1,0:T(8,128)(2,1)S(1)}, u32[]{:S(2)}, u32[]{:S(2)}) %collective-permute-start.1) | collective-permute-done | bytes 520224 | tf_op jit(solution)/shard_map/ppermute | solution.py:13
  48.6 0.2 maximum_select_fusion
  48.7 0.4 pad_maximum_fusion
  49.1 27.2 %fusion.3 = f32[2,128,2048]{2,0,1:T(2,128)S(1)} fusion(bf16[2,255,2048]{2,1,0:T(8,128)(2,1)S(1)} %pad_maximum_fusion, bf16[128,1,2048]{2,0,1:T(8,128)(2,1)S(1)} %bitcast.61), kind=kOutput, calls=%fused_computation.13 | convolution fusion | flops 134217728 | bytes 4710400 | tf_op jit(solution)/shard_map/conv_general_dilated | solution.py:19
  76.3 1.3 %multiply_convert_fusion = (bf16[2,128,2048]{2,1,0:T(8,128)(2,1)S(1)}, f32[2,128,2048]{2,1,0:T(8,128)S(1)}) fusion(f32[2,128,2048]{2,1,0:T(8,128)S(1)} %bitcast.49, f32[2,128,2048]{2,0,1:T(2,128)S(1)} %fusion.3), kind=kLoop, calls=%fused_computation.9 | loop fusion | flops 1048576 | bytes 7340032 | tf_op jit(solution)/shard_map/convert_element_type | solution.py:64
  77.6 0.4 fusion.8
  78.1 12.1 %psum.7 = f32[256,8]{0,1:T(8,128)S(1)} all-reduce(f32[256,8]{0,1:T(8,128)S(1)} %fusion.8), channel_id=1, replica_groups=mesh['seq'=8,'chan'=4] {'chan'}, use_global_device_ids=true, to_apply=%region_4.5 | all-reduce | flops 2048 | bytes 16384 | tf_op jit(solution)/shard_map/psum | solution.py:85
  90.2 1.7 %fusion.2 = bf16[256,2048]{1,0:T(8,128)(2,1)S(1)} fusion(f32[2,128,2048]{2,1,0:T(8,128)S(1)} %get-tuple-element.13, bf16[5,256,2048]{2,1,0:T(8,128)(2,1)} %param.7), kind=kLoop, calls=%fused_computation.8 | loop fusion | flops 1572864 | bytes 4194304 | tf_op jit(solution)/shard_map/convert_element_type | solution.py:64
  91.8 0.2 convolution_add_fusion
  92.0 2.1 %fusion.1 = bf16[256,2048]{1,0:T(8,128)(2,1)} fusion(bf16[256,2048]{1,0:T(8,128)(2,1)S(1)} %fusion.2, bf16[4,8,2048]{2,1,0:T(8,128)(2,1)S(1)} %bitcast.64, f32[256,4]{0,1:T(4,128)S(1)} %convolution_add_fusion, f32[256,4]{0,1:T(4,128)S(1)} %fusion.19), kind=kOutput, calls=%fused_computation.4 | convolution fusion | flops 102240256 | bytes 2170880 | tf_op jit(solution)/shard_map/dot_general | solution.py:95
  (15 shorter events, 0.1 us)
Async XLA Ops:
  0.0 40.4 %copy-start = (f32[16,4]{0,1:T(4,128)S(1)}, f32[16,4]{0,1:T(4,128)}, u32[]{:S(2)}) copy-start(f32[16,4]{0,1:T(4,128)} %param.11) | copy-start | bytes 772
  2.0 19.9 %collective-permute-start = (bf16[6,2048]{1,0:T(8,128)(2,1)S(1)}, bf16[6,2048]{1,0:T(8,128)(2,1)S(1)}, u32[]{:S(2)}, u32[]{:S(2)}) collective-permute-start(bf16[6,2048]{1,0:T(8,128)(2,1)S(1)} %slice_bitcast_fusion), channel_id=1, source_target_pairs={{0,4},{4,8},{8,12},{12,16},{16,20},{20,24},{24,28},{1,5},{5,9},{9,... | collective-permute-start | bytes 73736 | tf_op jit(solution)/shard_map/ppermute | solution.py:13
  3.9 6.4 %copy-start.8 = (s32[4]{0:T(128)S(1)}, s32[4]{0:T(128)}, u32[]{:S(2)}) copy-start(s32[4]{0:T(128)} %param.12) | copy-start | bytes 52
  3.9 6.8 %copy-start.5 = (bf16[2,8,2048]{2,1,0:T(8,128)(2,1)S(1)}, bf16[2,8,2048]{2,1,0:T(8,128)(2,1)}, u32[]{:S(2)}) copy-start(bf16[2,8,2048]{2,1,0:T(8,128)(2,1)} %param.10) | copy-start | bytes 196612
  3.9 17.0 %copy-start.7 = (s32[4]{0:T(128)S(1)}, s32[4]{0:T(128)}, u32[]{:S(2)}) copy-start(s32[4]{0:T(128)} %param.13) | copy-start | bytes 52
  10.3 11.1 %copy-start.6 = (bf16[7,2048]{1,0:T(8,128)(2,1)S(1)}, bf16[7,2048]{1,0:T(8,128)(2,1)}, u32[]{:S(2)}) copy-start(bf16[7,2048]{1,0:T(8,128)(2,1)} %param.8) | copy-start | bytes 86020
  24.3 4.1 %copy-start.9 = (pred[16,17]{0,1:T(8,128)(4,1)S(1)}, pred[16,17]{0,1:T(8,128)(4,1)}, u32[]{:S(2)}) copy-start(pred[16,17]{0,1:T(8,128)(4,1)} %constant.30) | copy-start | bytes 820
  32.7 3.7 %copy-start.2 = (f32[256,2048]{1,0:T(8,128)S(1)}, f32[256,2048]{1,0:T(8,128)}, u32[]{:S(2)}) copy-start(f32[256,2048]{1,0:T(8,128)} %get-tuple-element.6) | copy-start | bytes 6291460
  32.7 4.1 %copy-start.3 = (f32[256,2048]{1,0:T(8,128)S(1)}, f32[256,2048]{1,0:T(8,128)}, u32[]{:S(2)}) copy-start(f32[256,2048]{1,0:T(8,128)} %get-tuple-element.7) | copy-start | bytes 6291460
  36.4 3.3 %copy-start.4 = (bf16[128,2048]{1,0:T(8,128)(2,1)S(1)}, bf16[128,2048]{1,0:T(8,128)(2,1)}, u32[]{:S(2)}) copy-start(bf16[128,2048]{1,0:T(8,128)(2,1)} %param.9) | copy-start | bytes 1572868
  37.2 11.4 %collective-permute-start.1 = (bf16[127,2048]{1,0:T(8,128)(2,1)S(1)}, bf16[127,2048]{1,0:T(8,128)(2,1)S(1)}, u32[]{:S(2)}, u32[]{:S(2)}) collective-permute-start(bf16[127,2048]{1,0:T(8,128)(2,1)S(1)} %fusion.9), channel_id=1, source_target_pairs={{0,4},{4,8},{8,12},{12,16},{16,20},{20,24},{24,28},{1,5},{5,9},{9,... | collective-permute-start | bytes 1560584 | tf_op jit(solution)/shard_map/ppermute | solution.py:13
  49.1 27.2 %copy-start.1 = (f32[1,256,2048]{2,1,0:T(8,128)S(1)}, f32[1,256,2048]{2,1,0:T(8,128)}, u32[]{:S(2)}) copy-start(f32[1,256,2048]{2,1,0:T(8,128)} %get-tuple-element.5) | copy-start | bytes 6291460
where the time goes:
time: 94.4 us; the launch traced here: 94.1 us
  matrix products  31.8 us (34%)
  blocking collectives  22 us (23%)
  other arithmetic  20.6 us (22%)
  waiting for transfers between devices  7.82 us (8%)
  local copies, waits for them, and re-layouts  7.28 us (8%)
  starting transfers between devices  4.36 us (5%)
    conv_general_dilated x2, matrix products, depth_conv(): lax.conv_general_dilated(window, kernel, (1,), 'VALID', dimension_numbers...  28.6 us
    psum x1, blocking collectives, on_device(): summed = lax.psum(selected, 'chan')  12.1 us
    all_gather x1, blocking collectives, on_device(): all_rows = lax.all_gather(edit_table, 'seq', axis=0, tiled=True)  9.92 us
    convert_element_type x3, other arithmetic, on_device(): hidden = (second_gate.astype(jnp.float32) * long_out).astype(jnp.bfloat16)  9.31 us
    ppermute x2, waiting for transfers between devices, from_behind(): return lax.ppermute(block, axis, route)  7.82 us
    conv_general_dilated x2, other arithmetic, depth_conv(): lax.conv_general_dilated(window, kernel, (1,), 'VALID', dimension_numbers...  7.49 us
    ppermute x2, starting transfers between devices, from_behind(): return lax.ppermute(block, axis, route)  4.36 us
    conv_general_dilated x3, local copies, waits for them, and re-layouts, depth_conv(): lax.conv_general_dilated(window, kernel, (1,), 'VALID', dimension_numbers...  3.16 us
  transfers between devices with their start and end apart: 2, of which 1 were waited for; matrix products, arithmetic and copies ran while one was open for 10% of the time, Pallas kernels for 0%

commit v1 on v0

v1 whole, which is shorter than its diff:
```python
import functools

import jax
import jax.numpy as jnp
import ml_dtypes
import numpy as np
from jax import lax
from jax.experimental import pallas as pl
from jax.experimental.pallas import tpu as pltpu
from jax.sharding import PartitionSpec as P

TILE = 128
SEQS = 4
ROWS8 = 8
CHUNK = 512
LEAD = 16
BF16 = jnp.bfloat16
F32 = jnp.float32


def split_np(a):
    hi = a.astype(ml_dtypes.bfloat16)
    lo = (a - hi.astype(np.float64)).astype(ml_dtypes.bfloat16)
    return hi, lo


def transforms():
    ks = np.concatenate([np.arange(0, TILE, 2), np.arange(1, TILE, 2)])
    angle = np.pi * np.outer(ks + 0.5, np.arange(TILE)) / TILE
    hi, lo = split_np(np.concatenate([np.cos(angle), -np.sin(angle)], axis=0))
    forward = np.concatenate([hi, lo], axis=1)
    back = np.concatenate([np.cos(angle).T, -np.sin(angle).T], axis=1) / TILE
    hi, lo = split_np(back)
    return forward, np.concatenate([hi, lo], axis=0)


def halves(x):
    hi = x.astype(BF16)
    return hi, (x - hi.astype(F32)).astype(BF16)


def dot(a, b):
    return jnp.dot(a, b, preferred_element_type=F32)


def main_kernel(
    n_seq, n_chan, bits,
    streams, short_f, long_f, table, bias, tiles, tenant, fwd, inv,
    hid_out, coef_out, rows_out,
    s_buf, gwin, gsend, grecv, csend, crecv, cold, spec, hspec, hid, tfull, tlast, trecv, psend, precv,
    in_sem, out_sem, g_ss, g_rs, c_ss, c_rs, t_ss, t_rs, p_ss, p_rs,
):
    chunks = s_buf.shape[0]
    per = table.shape[0]
    phases = len(bits)
    me = lax.axis_index("seq")
    z = lax.axis_index("chan")
    after = lax.rem(me + 1, n_seq)
    before = lax.rem(me + n_seq - 1, n_seq)

    def partner(p):
        b = bits[p]
        return me + b - 2 * b * lax.rem(lax.div(me, b), 2)

    def peer(d):
        return lax.rem(z + d, n_chan)

    def cols(c):
        return pl.ds(pl.multiple_of(c * CHUNK, CHUNK), CHUNK)

    tail = pl.ds(TILE - LEAD, TILE + LEAD)
    head = pl.ds(0, TILE - LEAD)

    def load(c, part):
        rows = tail if part == 0 else head
        return pltpu.make_async_copy(
            streams.at[:, rows, cols(c)], s_buf.at[c, :, rows, :], in_sem.at[part, c]
        )

    for c in range(chunks):
        load(c, 0).start()
    for c in range(chunks):
        load(c, 1).start()

    barrier = pltpu.get_barrier_semaphore()
    greeted = [{"seq": after}, {"seq": before}]
    greeted += [{"seq": partner(p)} for p in range(phases)]
    greeted += [{"chan": peer(d)} for d in range(1, n_chan)]
    for who in greeted:
        pl.semaphore_signal(barrier, inc=1, device_id=who, device_id_type=pl.DeviceIdType.MESH)
    pl.semaphore_wait(barrier, len(greeted))

    def remote(src, dst, ss, rs, who):
        return pltpu.make_async_remote_copy(
            src_ref=src, dst_ref=dst, send_sem=ss, recv_sem=rs, device_id=who,
            device_id_type=pl.DeviceIdType.MESH,
        )

    def table_copy(p):
        src = tlast if p == phases - 1 else tfull.at[p]
        dst = trecv.at[p, pl.ds(0, 16)] if p == phases - 1 else trecv.at[p]
        return remote(src, dst, t_ss.at[p], t_rs.at[p], {"seq": partner(p)})

    def gate_copy(c):
        return remote(gsend.at[c], grecv.at[c], g_ss.at[c], g_rs.at[c], {"seq": after})

    def border_copy(c):
        return remote(csend.at[c], crecv.at[c], c_ss.at[c], c_rs.at[c], {"seq": after})

    def part_copy(i, d):
        return remote(
            psend.at[i], precv.at[i, d - 1], p_ss.at[i, d - 1], p_rs.at[i, d - 1], {"chan": peer(d)}
        )

    ends = []
    for s in range(SEQS):
        ends.append(tiles[s] if s == 0 else ends[-1] + tiles[s])

    def seq_of(tile):
        return sum(jnp.where(e <= tile, 1, 0) for e in ends)

    def joined(tile):
        hits = sum(jnp.where(e == tile, 1, 0) for e in ends) + jnp.where(tile == 0, 1, 0)
        return jnp.where(hits > 0, 0.0, 1.0).astype(F32)

    join0, join1 = joined(2 * me), joined(2 * me + 1)

    def pick_tiles(src, who):
        picked = []
        for i in range(2):
            s_of = seq_of(2 * who + i)
            total = jnp.zeros((ROWS8, src.shape[1]), F32)
            for s in range(SEQS):
                total += jnp.where(s_of == s, 1.0, 0.0).astype(F32) * src[ROWS8 * s : ROWS8 * (s + 1)]
            picked.append(total)
        return jnp.concatenate(picked, axis=0)

    for c in range(chunks):
        at = slice(c * CHUNK, (c + 1) * CHUNK)
        owned = [table[k, :, at].astype(F32) for k in range(per)]
        out = []
        for s in range(SEQS):
            total = jnp.zeros((ROWS8, CHUNK), F32)
            for k in range(per):
                total += jnp.where(tenant[s] == per * me + k, 1.0, 0.0).astype(F32) * owned[k]
            out.append(total)
        tfull[0, :, at] = jnp.concatenate(out, axis=0).astype(BF16)
    if phases > 1:
        table_copy(0).start()

    def carry(c, i, dst, lead):
        base = TILE * i
        gwin[0:LEAD] = lead
        key = s_buf[c, 1, pl.ds(base, TILE), :].astype(F32)
        val = s_buf[c, 2, pl.ds(base, TILE), :].astype(F32)
        gated = (key * val).astype(BF16)
        if i == 1:
            gsend[c] = gated[TILE - LEAD :]
            gate_copy(c).start()
        gwin[LEAD:] = gated.astype(F32)
        taps = short_f[:, cols(c)].astype(F32)
        for b in range(CHUNK // 128):
            at = slice(128 * b, 128 * (b + 1))
            total = jnp.zeros((TILE, 128), F32)
            for j in range(short_f.shape[0]):
                total += taps[j : j + 1, at] * gwin[LEAD - j : LEAD - j + TILE, at]
            gate = s_buf[c, 0, pl.ds(base, TILE), at].astype(F32)
            mixed = (gate * total).astype(BF16).astype(F32)
            key2 = s_buf[c, 4, pl.ds(base, TILE), at].astype(F32)
            dst[c, :, at] = (key2 * mixed).astype(BF16)

    def table_step(p):
        table_copy(p).wait()
        total = tfull[p].astype(F32) + trecv[p].astype(F32)
        tfull[p + 1] = total.astype(BF16)
        if p + 1 < phases - 1:
            table_copy(p + 1).start()
        else:
            tlast[...] = pick_tiles(total, partner(phases - 1)).astype(BF16)
            table_copy(phases - 1).start()

    def tail_chunk(c, _):
        load(c, 0).wait()
        near = pl.ds(TILE - LEAD, LEAD)
        lead = (s_buf[c, 1, near, :].astype(F32) * s_buf[c, 2, near, :].astype(F32)).astype(BF16)
        carry(c, 1, csend, lead.astype(F32) * join1)
        border_copy(c).start()
        return 0

    lax.fori_loop(0, chunks, tail_chunk, 0)

    if phases == 1:
        tlast[...] = pick_tiles(tfull[0].astype(F32), partner(0)).astype(BF16)
        table_copy(0).start()
    if phases > 1:
        table_step(0)

    def twice(x):
        return jnp.concatenate([x, x], axis=0)

    def transform_chunk(c, _):
        hspec[c] = dot(fwd[...], twice(long_f[:, cols(c)]))
        spec[1, c] = dot(fwd[...], twice(csend[c]))
        return 0

    lax.fori_loop(0, chunks, transform_chunk, 0)
    for p in range(1, phases - 1):
        table_step(p)

    def head_chunk(c, _):
        load(c, 1).wait()
        gate_copy(c).wait_recv()
        carry(c, 0, cold, grecv[c].astype(F32) * join0)
        spec[0, c] = dot(fwd[...], twice(cold[c]))
        return 0

    lax.fori_loop(0, chunks, head_chunk, 0)

    table_copy(phases - 1).wait()
    mine = pick_tiles(tfull[phases - 1].astype(F32), me) + trecv[phases - 1, 0:16].astype(F32)
    rows_out[...] = mine.astype(BF16)

    half, quarter = TILE, TILE // 2

    def finish(c, i, prev, join):
        pre, pim = prev[:half] * join, prev[half:] * join
        cre, cim = spec[i, c, 0:half], spec[i, c, half:]
        gre = jnp.concatenate([cre[:quarter] - pim[:quarter], cre[quarter:] + pim[quarter:]], axis=0)
        gim = jnp.concatenate([cim[:quarter] + pre[:quarter], cim[quarter:] - pre[quarter:]], axis=0)
        hre, him = hspec[c, 0:half], hspec[c, half:]
        hi, lo = halves(jnp.concatenate([hre * gre - him * gim, hre * gim + him * gre], axis=0))
        both = dot(inv[...], hi)
        long_out = both[:TILE] + both[TILE:] + dot(inv[0:TILE], lo)
        base = TILE * i
        gate = s_buf[c, 3, pl.ds(base, TILE), :].astype(F32)
        hidden = (gate * long_out).astype(BF16)
        hid[c, pl.ds(base, TILE), :] = hidden
        write(c, i).start()
        return lax.dot_general(
            rows_out[:, cols(c)], hidden, (((1,), (1,)), ((), ())), preferred_element_type=F32
        )

    def write(c, i):
        rows = pl.ds(TILE * i, TILE)
        return pltpu.make_async_copy(
            hid.at[c, rows, :], hid_out.at[rows, cols(c)], out_sem.at[i, c]
        )

    def share(i, projected):
        mine = projected[ROWS8 * i : ROWS8 * (i + 1)]
        rank = ROWS8 // 2
        delta = mine[rank:] - mine[:rank]
        psend[i] = jnp.concatenate([delta, jnp.zeros_like(delta)], axis=0)
        for d in range(1, n_chan):
            part_copy(i, d).start()

    zero = jnp.zeros((2 * ROWS8, TILE), F32)
    share(1, lax.fori_loop(0, chunks, lambda c, t: t + finish(c, 1, spec[0, c], join1), zero))

    def border_chunk(c, t):
        border_copy(c).wait_recv()
        return t + finish(c, 0, dot(fwd[...], twice(crecv[c])), join0)

    share(0, lax.fori_loop(0, chunks, border_chunk, zero))

    coef_out[...] = jnp.zeros_like(coef_out)
    row = lax.broadcasted_iota(jnp.int32, (ROWS8, TILE), 0)
    for i in (1, 0):
        s_of = seq_of(2 * me + i)
        owner = tenant[0]
        for s in range(1, SEQS):
            owner = jnp.where(s_of == s, tenant[s], owner)
        total = psend[i]
        for r in range(ROWS8 // 2):
            total += jnp.where(row == r, bias[owner, r], 0.0)
        for d in range(1, n_chan):
            part_copy(i, d).wait()
            total += precv[i, d - 1]
        coef_out[ROWS8 * i : ROWS8 * (i + 1), TILE * i : TILE * (i + 1)] = total

    def drain(c, _):
        gate_copy(c).wait_send()
        border_copy(c).wait_send()
        write(c, 0).wait()
        write(c, 1).wait()
        return 0

    lax.fori_loop(0, chunks, drain, 0)


def edit_kernel(hid, coef, rows, out):
    hi, lo = halves(coef[...])
    change = lax.dot_general(
        jnp.concatenate([hi, lo], axis=0),
        jnp.concatenate([rows[...], rows[...]], axis=0),
        (((0,), (0,)), ((), ())),
        preferred_element_type=F32,
    )
    out[...] = (hid[...].astype(F32) + change).astype(BF16)


def on_device(n_seq, n_chan, streams, short_f, long_f, table, bias, tiles, tenant):
    rows, width = streams.shape[1:]
    chunks = width // CHUNK
    bits = [1 << b for b in range(n_seq.bit_length() - 1)]
    bits = bits[2:] + bits[:1] + bits[1:2]
    phases = len(bits)
    fwd, inv = transforms()
    vmem = pl.BlockSpec(memory_space=pltpu.VMEM)
    smem = pl.BlockSpec(memory_space=pltpu.SMEM)
    hbm = pl.BlockSpec(memory_space=pl.ANY)
    dma = pltpu.SemaphoreType.DMA
    hidden, coef, picked = pl.pallas_call(
        functools.partial(main_kernel, n_seq, n_chan, bits),
        out_shape=(
            jax.ShapeDtypeStruct((rows, width), BF16),
            jax.ShapeDtypeStruct((2 * ROWS8, rows), F32),
            jax.ShapeDtypeStruct((2 * ROWS8, width), BF16),
        ),
        in_specs=[hbm, vmem, vmem, vmem, smem, smem, smem, vmem, vmem],
        out_specs=(hbm, vmem, vmem),
        scratch_shapes=[
            pltpu.VMEM((chunks, 5, rows, CHUNK), BF16),
            pltpu.VMEM((LEAD + TILE, CHUNK), F32),
            pltpu.VMEM((chunks, LEAD, CHUNK), BF16),
            pltpu.VMEM((chunks, LEAD, CHUNK), BF16),
            pltpu.VMEM((chunks, TILE, CHUNK), BF16),
            pltpu.VMEM((chunks, TILE, CHUNK), BF16),
            pltpu.VMEM((chunks, TILE, CHUNK), BF16),
            pltpu.VMEM((2, chunks, 2 * TILE, CHUNK), F32),
            pltpu.VMEM((chunks, 2 * TILE, CHUNK), F32),
            pltpu.VMEM((chunks, rows, CHUNK), BF16),
            pltpu.VMEM((phases, SEQS * ROWS8, width), BF16),
            pltpu.VMEM((2 * ROWS8, width), BF16),
            pltpu.VMEM((phases, SEQS * ROWS8, width), BF16),
            pltpu.VMEM((2, ROWS8, TILE), F32),
            pltpu.VMEM((2, n_chan - 1, ROWS8, TILE), F32),
            dma((2, chunks)),
            dma((2, chunks)),
            dma((chunks,)),
            dma((chunks,)),
            dma((chunks,)),
            dma((chunks,)),
            dma((phases,)),
            dma((phases,)),
            dma((2, n_chan - 1)),
            dma((2, n_chan - 1)),
        ],
        compiler_params=pltpu.CompilerParams(
            collective_id=0, has_side_effects=True, vmem_limit_bytes=40 * 2**20
        ),
    )(streams, short_f, long_f, table, bias, tiles, tenant, jnp.asarray(fwd), jnp.asarray(inv))
    return pl.pallas_call(
        edit_kernel,
        grid=(chunks,),
        out_shape=jax.ShapeDtypeStruct((rows, width), BF16),
        in_specs=[
            pl.BlockSpec((rows, CHUNK), lambda c: (0, c)),
            pl.BlockSpec((2 * ROWS8, rows), lambda c: (0, 0)),
            pl.BlockSpec((2 * ROWS8, CHUNK), lambda c: (0, c)),
        ],
        out_specs=pl.BlockSpec((rows, CHUNK), lambda c: (0, c)),
    )(hidden, coef, picked)


def solution(mesh):
    in_specs = (
        P(None, "seq", "chan"),
        P(None, "chan"),
        P(None, "chan"),
        P("seq", None, "chan"),
        P(),
        P(),
        P(),
    )
    body = functools.partial(on_device, mesh.shape["seq"], mesh.shape["chan"])
    return jax.shard_map(
        body, mesh=mesh, in_specs=in_specs, out_specs=P("seq", "chan"), check_vma=False
    )
```

time: 94.4 us -> 45.9 us (0.49)
  the two profiles are of different devices: /device:TPU:4 before, /device:TPU:0 now
where the time goes in v1:
time: 45.9 us; the launch traced here: 45.5 us
  Pallas kernels  34.3 us (75%)
  local copies, waits for them, and re-layouts  11.2 us (24%)
    pallas_call x1, Pallas kernels, on_device(): pl.pallas_call(functools.partial(main_kernel, n_seq, n_chan, bits), out_s...  30.4 us
    unnamed x23, local copies, waits for them, and re-layouts  11.2 us
    pallas_call x1, Pallas kernels, on_device(): pl.pallas_call(edit_kernel, grid=(chunks,), out_shape=jax.ShapeDtypeStruc...  3.83 us

profile of v1, /device:TPU:0, one launch (start us, length us, event | category | flops | bytes accessed | tf_op | source)
XLA Modules:
  0.0 45.5 jit_solution(3990977354043566876)
XLA Ops:
  0.0 0.8 %copy.10.bias = f32[16,4]{1,0:T(8,128)S(1)} copy(f32[16,4]{0,1:T(4,128)} %param.13) | data formatting | bytes 512 | tf_op args[4]
  0.8 0.0 copy-start
  0.8 2.5 %copy-done = bf16[5,256,2048]{2,1,0:T(8,128)(2,1)S(1)} copy-done((bf16[5,256,2048]{2,1,0:T(8,128)(2,1)S(1)}, bf16[5,256,2048]{2,1,0:T(8,128)(2,1)}, u32[]{:S(2)}) %copy-start) | copy-done | bytes 5242904
  3.2 0.0 copy-start.2
  3.2 1.0 %copy-done.2 = bf16[128,2048]{1,0:T(8,128)(2,1)S(1)} copy-done((bf16[128,2048]{1,0:T(8,128)(2,1)S(1)}, bf16[128,2048]{1,0:T(8,128)(2,1)}, u32[]{:S(2)}) %copy-start.2) | copy-done | bytes 524312
  4.3 0.0 copy-start.3
  4.3 0.9 %copy-done.3 = bf16[256,256]{1,0:T(8,128)(2,1)S(1)} copy-done((bf16[256,256]{1,0:T(8,128)(2,1)S(1)}, bf16[256,256]{1,0:T(8,128)(2,1)}, u32[]{:S(2)}) %copy-start.3) | copy-done | bytes 131096
  5.2 0.0 copy-start.4
  5.2 0.9 %copy-done.4 = bf16[256,256]{1,0:T(8,128)(2,1)S(1)} copy-done((bf16[256,256]{1,0:T(8,128)(2,1)S(1)}, bf16[256,256]{1,0:T(8,128)(2,1)}, u32[]{:S(2)}) %copy-start.4) | copy-done | bytes 131096
  6.1 0.0 copy-start.5
  6.1 0.8 %copy-done.5 = bf16[2,8,2048]{2,1,0:T(8,128)(2,1)S(1)} copy-done((bf16[2,8,2048]{2,1,0:T(8,128)(2,1)S(1)}, bf16[2,8,2048]{2,1,0:T(8,128)(2,1)}, u32[]{:S(2)}) %copy-start.5) | copy-done | bytes 65560
  6.9 0.0 copy-start.7
  6.9 0.8 %copy-done.7 = bf16[7,2048]{1,0:T(8,128)(2,1)S(1)} copy-done((bf16[7,2048]{1,0:T(8,128)(2,1)S(1)}, bf16[7,2048]{1,0:T(8,128)(2,1)}, u32[]{:S(2)}) %copy-start.7) | copy-done | bytes 28696
  7.7 0.0 copy-start.9
  7.7 0.7 %copy-done.9 = s32[4]{0:T(128)S(1)} copy-done((s32[4]{0:T(128)S(1)}, s32[4]{0:T(128)}, u32[]{:S(2)}) %copy-start.9) | copy-done | bytes 40
  8.4 0.0 copy-start.10
  8.4 0.7 %copy-done.10 = s32[4]{0:T(128)S(1)} copy-done((s32[4]{0:T(128)S(1)}, s32[4]{0:T(128)}, u32[]{:S(2)}) %copy-start.10) | copy-done | bytes 40
  9.0 30.4 %shard_map.91 = (bf16[256,2048]{1,0:T(8,128)(2,1)S(1)}, f32[16,256]{1,0:T(8,128)S(1)}, bf16[16,2048]{1,0:T(8,128)(2,1)S(1)}) custom-call(bf16[5,256,2048]{2,1,0:T(8,128)(2,1)S(1)} %copy-done, bf16[7,2048]{1,0:T(8,128)(2,1)S(1)} %copy-done.7, bf16[128,2048]{1,0:T(8,128)(2,1)S(1)} %copy-done.2, bf16[2,8,2048]{2,1,0:T(8,128)(2,1)S(1)} %copy-done.5, ...), custom_call_target="tpu_custom_call" | custom-call | tf_op jit(solution)/shard_map/pallas_call | solution.py:313
  39.4 0.0 copy-start.1
  39.4 1.0 %copy-done.1 = bf16[256,2048]{1,0:T(8,128)(2,1)} copy-done((bf16[256,2048]{1,0:T(8,128)(2,1)}, bf16[256,2048]{1,0:T(8,128)(2,1)S(1)}, u32[]{:S(2)}) %copy-start.1) | copy-done | bytes 1048600
  40.4 0.0 copy-start.6
  40.4 0.6 %copy-done.6 = bf16[16,2048]{1,0:T(8,128)(2,1)} copy-done((bf16[16,2048]{1,0:T(8,128)(2,1)}, bf16[16,2048]{1,0:T(8,128)(2,1)S(1)}, u32[]{:S(2)}) %copy-start.6) | copy-done | bytes 65560
  41.0 0.0 copy-start.8
  41.0 0.6 %copy-done.8 = f32[16,256]{1,0:T(8,128)} copy-done((f32[16,256]{1,0:T(8,128)}, f32[16,256]{1,0:T(8,128)S(1)}, u32[]{:S(2)}) %copy-start.8) | copy-done | bytes 16408
  41.6 3.8 %shard_map.92 = bf16[256,2048]{1,0:T(8,128)(2,1)} custom-call(bf16[256,2048]{1,0:T(8,128)(2,1)} %copy-done.1, f32[16,256]{1,0:T(8,128)} %copy-done.8, bf16[16,2048]{1,0:T(8,128)(2,1)} %copy-done.6), custom_call_target="tpu_custom_call" | custom-call | tf_op jit(solution)/shard_map/pallas_call | solution.py:353
Async XLA Ops:
  0.8 2.5 %copy-start = (bf16[5,256,2048]{2,1,0:T(8,128)(2,1)S(1)}, bf16[5,256,2048]{2,1,0:T(8,128)(2,1)}, u32[]{:S(2)}) copy-start(bf16[5,256,2048]{2,1,0:T(8,128)(2,1)} %streams.1) | copy-start | bytes 15728644
  3.2 1.0 %copy-start.2 = (bf16[128,2048]{1,0:T(8,128)(2,1)S(1)}, bf16[128,2048]{1,0:T(8,128)(2,1)}, u32[]{:S(2)}) copy-start(bf16[128,2048]{1,0:T(8,128)(2,1)} %long_f.1) | copy-start | bytes 1572868
  4.3 0.9 %copy-start.3 = (bf16[256,256]{1,0:T(8,128)(2,1)S(1)}, bf16[256,256]{1,0:T(8,128)(2,1)}, u32[]{:S(2)}) copy-start(bf16[256,256]{1,0:T(8,128)(2,1)} %constant.5.clone.inv) | copy-start | bytes 393220
  5.2 0.9 %copy-start.4 = (bf16[256,256]{1,0:T(8,128)(2,1)S(1)}, bf16[256,256]{1,0:T(8,128)(2,1)}, u32[]{:S(2)}) copy-start(bf16[256,256]{1,0:T(8,128)(2,1)} %constant.4.clone.fwd) | copy-start | bytes 393220
  6.1 0.8 %copy-start.5 = (bf16[2,8,2048]{2,1,0:T(8,128)(2,1)S(1)}, bf16[2,8,2048]{2,1,0:T(8,128)(2,1)}, u32[]{:S(2)}) copy-start(bf16[2,8,2048]{2,1,0:T(8,128)(2,1)} %table.1) | copy-start | bytes 196612
  6.9 0.8 %copy-start.7 = (bf16[7,2048]{1,0:T(8,128)(2,1)S(1)}, bf16[7,2048]{1,0:T(8,128)(2,1)}, u32[]{:S(2)}) copy-start(bf16[7,2048]{1,0:T(8,128)(2,1)} %short_f.1) | copy-start | bytes 86020
  7.7 0.7 %copy-start.9 = (s32[4]{0:T(128)S(1)}, s32[4]{0:T(128)}, u32[]{:S(2)}) copy-start(s32[4]{0:T(128)} %tiles.1) | copy-start | bytes 52
  8.4 0.7 %copy-start.10 = (s32[4]{0:T(128)S(1)}, s32[4]{0:T(128)}, u32[]{:S(2)}) copy-start(s32[4]{0:T(128)} %tenant.1) | copy-start | bytes 52
  39.4 1.0 %copy-start.1 = (bf16[256,2048]{1,0:T(8,128)(2,1)}, bf16[256,2048]{1,0:T(8,128)(2,1)S(1)}, u32[]{:S(2)}) copy-start(bf16[256,2048]{1,0:T(8,128)(2,1)S(1)} %get-tuple-element.8.hid) | copy-start | bytes 3145732
  40.4 0.6 %copy-start.6 = (bf16[16,2048]{1,0:T(8,128)(2,1)}, bf16[16,2048]{1,0:T(8,128)(2,1)S(1)}, u32[]{:S(2)}) copy-start(bf16[16,2048]{1,0:T(8,128)(2,1)S(1)} %get-tuple-element.10.rows) | copy-start | bytes 196612
  41.0 0.6 %copy-start.8 = (f32[16,256]{1,0:T(8,128)}, f32[16,256]{1,0:T(8,128)S(1)}, u32[]{:S(2)}) copy-start(f32[16,256]{1,0:T(8,128)S(1)} %get-tuple-element.9.coef) | copy-start | bytes 49156

commit v2 on v1

--- a/solution.py
+++ b/solution.py
@@ -45,10 +45,11 @@
 
 def main_kernel(
     n_seq, n_chan, bits,
-    streams, short_f, long_f, table, bias, tiles, tenant, fwd, inv,
-    hid_out, coef_out, rows_out,
-    s_buf, gwin, gsend, grecv, csend, crecv, cold, spec, hspec, hid, tfull, tlast, trecv, psend, precv,
-    in_sem, out_sem, g_ss, g_rs, c_ss, c_rs, t_ss, t_rs, p_ss, p_rs,
+    streams, short_h, long_h, table_h, bias, tiles, tenant, fwd_h, inv_h,
+    out,
+    short_f, long_f, table, fwd, inv, rows_own,
+    s_buf, gwin, gsend, grecv, csend, crecv, cold, spec, hspec, tfull, tlast, trecv, psend, precv,
+    in_sem, side_sem, g_ss, g_rs, c_ss, c_rs, t_ss, t_rs, p_ss, p_rs,
 ):
     chunks = s_buf.shape[0]
     per = table.shape[0]
@@ -77,8 +78,18 @@
             streams.at[:, rows, cols(c)], s_buf.at[c, :, rows, :], in_sem.at[part, c]
         )
 
+    sides = [
+        pltpu.make_async_copy(src, dst, side_sem.at[k])
+        for k, (src, dst) in enumerate(
+            ((table_h, table), (short_h, short_f), (fwd_h, fwd), (long_h, long_f), (inv_h, inv))
+        )
+    ]
+    sides[0].start()
+    sides[1].start()
     for c in range(chunks):
         load(c, 0).start()
+    for k in (2, 3, 4):
+        sides[k].start()
     for c in range(chunks):
         load(c, 1).start()
 
@@ -135,35 +146,38 @@
             picked.append(total)
         return jnp.concatenate(picked, axis=0)
 
+    sides[0].wait()
     for c in range(chunks):
         at = slice(c * CHUNK, (c + 1) * CHUNK)
         owned = [table[k, :, at].astype(F32) for k in range(per)]
-        out = []
+        by_seq = []
         for s in range(SEQS):
             total = jnp.zeros((ROWS8, CHUNK), F32)
             for k in range(per):
                 total += jnp.where(tenant[s] == per * me + k, 1.0, 0.0).astype(F32) * owned[k]
-            out.append(total)
-        tfull[0, :, at] = jnp.concatenate(out, axis=0).astype(BF16)
+            by_seq.append(total)
+        tfull[0, :, at] = jnp.concatenate(by_seq, axis=0).astype(BF16)
     if phases > 1:
         table_copy(0).start()
 
     def carry(c, i, dst, lead):
         base = TILE * i
-        gwin[0:LEAD] = lead
+        for b in range(CHUNK // 128):
+            gwin[b, 0:LEAD] = lead[:, 128 * b : 128 * (b + 1)]
         key = s_buf[c, 1, pl.ds(base, TILE), :].astype(F32)
         val = s_buf[c, 2, pl.ds(base, TILE), :].astype(F32)
         gated = (key * val).astype(BF16)
         if i == 1:
             gsend[c] = gated[TILE - LEAD :]
             gate_copy(c).start()
-        gwin[LEAD:] = gated.astype(F32)
+        for b in range(CHUNK // 128):
+            gwin[b, LEAD:] = gated[:, 128 * b : 128 * (b + 1)].astype(F32)
         taps = short_f[:, cols(c)].astype(F32)
         for b in range(CHUNK // 128):
             at = slice(128 * b, 128 * (b + 1))
             total = jnp.zeros((TILE, 128), F32)
             for j in range(short_f.shape[0]):
-                total += taps[j : j + 1, at] * gwin[LEAD - j : LEAD - j + TILE, at]
+                total += taps[j : j + 1, at] * gwin[b, LEAD - j : LEAD - j + TILE]
             gate = s_buf[c, 0, pl.ds(base, TILE), at].astype(F32)
             mixed = (gate * total).astype(BF16).astype(F32)
             key2 = s_buf[c, 4, pl.ds(base, TILE), at].astype(F32)
@@ -187,6 +201,7 @@
         border_copy(c).start()
         return 0
 
+    sides[1].wait()
     lax.fori_loop(0, chunks, tail_chunk, 0)
 
     if phases == 1:
@@ -203,6 +218,8 @@
         spec[1, c] = dot(fwd[...], twice(csend[c]))
         return 0
 
+    for k in (2, 3, 4):
+        sides[k].wait()
     lax.fori_loop(0, chunks, transform_chunk, 0)
     for p in range(1, phases - 1):
         table_step(p)
@@ -218,7 +235,7 @@
 
     table_copy(phases - 1).wait()
     mine = pick_tiles(tfull[phases - 1].astype(F32), me) + trecv[phases - 1, 0:16].astype(F32)
-    rows_out[...] = mine.astype(BF16)
+    rows_own[...] = mine.astype(BF16)
 
     half, quarter = TILE, TILE // 2
 
@@ -234,16 +251,9 @@
         base = TILE * i
         gate = s_buf[c, 3, pl.ds(base, TILE), :].astype(F32)
         hidden = (gate * long_out).astype(BF16)
-        hid[c, pl.ds(base, TILE), :] = hidden
-        write(c, i).start()
+        out[pl.ds(base, TILE), cols(c)] = hidden
         return lax.dot_general(
-            rows_out[:, cols(c)], hidden, (((1,), (1,)), ((), ())), preferred_element_type=F32
-        )
-
-    def write(c, i):
-        rows = pl.ds(TILE * i, TILE)
-        return pltpu.make_async_copy(
-            hid.at[c, rows, :], hid_out.at[rows, cols(c)], out_sem.at[i, c]
+            rows_own[:, cols(c)], hidden, (((1,), (1,)), ((), ())), preferred_element_type=F32
         )
 
     def share(i, projected):
@@ -263,7 +273,6 @@
 
     share(0, lax.fori_loop(0, chunks, border_chunk, zero))
 
-    coef_out[...] = jnp.zeros_like(coef_out)
     row = lax.broadcasted_iota(jnp.int32, (ROWS8, TILE), 0)
     for i in (1, 0):
         s_of = seq_of(2 * me + i)
@@ -272,31 +281,29 @@
             owner = jnp.where(s_of == s, tenant[s], owner)
         total = psend[i]
         for r in range(ROWS8 // 2):
-            total += jnp.where(row == r, bias[owner, r], 0.0)
+            total += jnp.where(row == r, bias[r, owner], 0.0)
         for d in range(1, n_chan):
             part_copy(i, d).wait()
             total += precv[i, d - 1]
-        coef_out[ROWS8 * i : ROWS8 * (i + 1), TILE * i : TILE * (i + 1)] = total
+        blank = jnp.zeros_like(total)
+        total = jnp.concatenate([total, blank] if i == 0 else [blank, total], axis=0)
+        hi, lo = halves(jnp.concatenate([total, jnp.zeros((TILE - 2 * ROWS8, TILE), F32)], axis=0).T)
+        spread = jnp.concatenate([hi[:, : 2 * ROWS8], lo[:, : 2 * ROWS8]], axis=1)
+        rows = slice(TILE * i, TILE * (i + 1))
+
+        def edit_chunk(c, _):
+            change = dot(spread, twice(rows_own[:, cols(c)]))
+            out[rows, cols(c)] = (out[rows, cols(c)].astype(F32) + change).astype(BF16)
+            return 0
+
+        lax.fori_loop(0, chunks, edit_chunk, 0)
 
     def drain(c, _):
         gate_copy(c).wait_send()
         border_copy(c).wait_send()
-        write(c, 0).wait()
-        write(c, 1).wait()
         return 0
 
     lax.fori_loop(0, chunks, drain, 0)
-
-
-def edit_kernel(hid, coef, rows, out):
-    hi, lo = halves(coef[...])
-    change = lax.dot_general(
-        jnp.concatenate([hi, lo], axis=0),
-        jnp.concatenate([rows[...], rows[...]], axis=0),
-        (((0,), (0,)), ((), ())),
-        preferred_element_type=F32,
-    )
-    out[...] = (hid[...].astype(F32) + change).astype(BF16)
 
 
 def on_device(n_seq, n_chan, streams, short_f, long_f, table, bias, tiles, tenant):
@@ -308,20 +315,22 @@
     fwd, inv = transforms()
     vmem = pl.BlockSpec(memory_space=pltpu.VMEM)
     smem = pl.BlockSpec(memory_space=pltpu.SMEM)
-    hbm = pl.BlockSpec(memory_space=pl.ANY)
+    hbm = pl.BlockSpec(memory_space=pltpu.HBM)
     dma = pltpu.SemaphoreType.DMA
-    hidden, coef, picked = pl.pallas_call(
+    return pl.pallas_call(
         functools.partial(main_kernel, n_seq, n_chan, bits),
-        out_shape=(
-            jax.ShapeDtypeStruct((rows, width), BF16),
-            jax.ShapeDtypeStruct((2 * ROWS8, rows), F32),
-            jax.ShapeDtypeStruct((2 * ROWS8, width), BF16),
-        ),
-        in_specs=[hbm, vmem, vmem, vmem, smem, smem, smem, vmem, vmem],
-        out_specs=(hbm, vmem, vmem),
+        out_shape=jax.ShapeDtypeStruct((rows, width), BF16),
+        in_specs=[hbm, hbm, hbm, hbm, smem, smem, smem, hbm, hbm],
+        out_specs=vmem,
         scratch_shapes=[
+            pltpu.VMEM(short_f.shape, BF16),
+            pltpu.VMEM(long_f.shape, BF16),
+            pltpu.VMEM(table.shape, BF16),
+            pltpu.VMEM(fwd.shape, BF16),
+            pltpu.VMEM(inv.shape, BF16),
+            pltpu.VMEM((2 * ROWS8, width), BF16),
             pltpu.VMEM((chunks, 5, rows, CHUNK), BF16),
-            pltpu.VMEM((LEAD + TILE, CHUNK), F32),
+            pltpu.VMEM((CHUNK // 128, LEAD + TILE, 128), F32),
             pltpu.VMEM((chunks, LEAD, CHUNK), BF16),
             pltpu.VMEM((chunks, LEAD, CHUNK), BF16),
             pltpu.VMEM((chunks, TILE, CHUNK), BF16),
@@ -329,14 +338,13 @@
             pltpu.VMEM((chunks, TILE, CHUNK), BF16),
             pltpu.VMEM((2, chunks, 2 * TILE, CHUNK), F32),
             pltpu.VMEM((chunks, 2 * TILE, CHUNK), F32),
-            pltpu.VMEM((chunks, rows, CHUNK), BF16),
             pltpu.VMEM((phases, SEQS * ROWS8, width), BF16),
             pltpu.VMEM((2 * ROWS8, width), BF16),
             pltpu.VMEM((phases, SEQS * ROWS8, width), BF16),
             pltpu.VMEM((2, ROWS8, TILE), F32),
             pltpu.VMEM((2, n_chan - 1, ROWS8, TILE), F32),
             dma((2, chunks)),
-            dma((2, chunks)),
+            dma((5,)),
             dma((chunks,)),
             dma((chunks,)),
             dma((chunks,)),
@@ -347,20 +355,9 @@
             dma((2, n_chan - 1)),
         ],
         compiler_params=pltpu.CompilerParams(
-            collective_id=0, has_side_effects=True, vmem_limit_bytes=40 * 2**20
+            collective_id=0, has_side_effects=True, vmem_limit_bytes=56 * 2**20
         ),
-    )(streams, short_f, long_f, table, bias, tiles, tenant, jnp.asarray(fwd), jnp.asarray(inv))
-    return pl.pallas_call(
-        edit_kernel,
-        grid=(chunks,),
-        out_shape=jax.ShapeDtypeStruct((rows, width), BF16),
-        in_specs=[
-            pl.BlockSpec((rows, CHUNK), lambda c: (0, c)),
-            pl.BlockSpec((2 * ROWS8, rows), lambda c: (0, 0)),
-            pl.BlockSpec((2 * ROWS8, CHUNK), lambda c: (0, c)),
-        ],
-        out_specs=pl.BlockSpec((rows, CHUNK), lambda c: (0, c)),
-    )(hidden, coef, picked)
+    )(streams, short_f, long_f, table, bias.T, tiles, tenant, jnp.asarray(fwd), jnp.asarray(inv))
 
 
 def solution(mesh):

time: 45.9 us -> 33.2 us (0.72)
  local copies, waits for them, and re-layouts: 11.2 us -> 2.3 us
  Pallas kernels: 34.3 us -> 30.7 us
    unnamed x23 -> x1, local copies, waits for them, and re-layouts: 11.2 us -> 2.3 us
    pallas_call x1 -> x0, Pallas kernels: 3.83 us -> none  [on_device(): pl.pallas_call(edit_kernel, grid=(chunks,), out_shape=jax.ShapeDtypeStruc...]
where the time goes in v2:
time: 33.2 us; the launch traced here: 33 us
  Pallas kernels  30.7 us (92%)
  local copies, waits for them, and re-layouts  2.3 us (7%)
    pallas_call x1, Pallas kernels, on_device(): pl.pallas_call(functools.partial(main_kernel, n_seq, n_chan, bits), out_s...  30.7 us
    unnamed x1, local copies, waits for them, and re-layouts  2.3 us

profile of v2, /device:TPU:0, one launch (start us, length us, event | category | flops | bytes accessed | tf_op | source)
XLA Modules:
  0.0 33.0 jit_solution(15863272722029219234)
XLA Ops:
  0.0 30.7 %shard_map.91 = bf16[256,2048]{1,0:T(8,128)(2,1)} custom-call(bf16[5,256,2048]{2,1,0:T(8,128)(2,1)} %streams.1, bf16[7,2048]{1,0:T(8,128)(2,1)} %short_h.1, bf16[128,2048]{1,0:T(8,128)(2,1)} %long_h.1, bf16[2,8,2048]{2,1,0:T(8,128)(2,1)} %table_h.1, f32[4,16]{1,0:T(4,128)} %bitcast.1, s32[4]{0:T(128)} %tiles.1, s32[4]{0:T(128)} %tenant.1, ...), custom_call_target="tpu_custom_call" | custom-call | tf_op jit(solution)/shard_map/pallas_call | solution.py:320
  30.7 2.3 %copy.11 = bf16[256,2048]{1,0:T(8,128)(2,1)} copy(bf16[256,2048]{1,0:T(8,128)(2,1)} %shard_map.91) | data formatting | bytes 2097152
